TPU v7x, 512 devices: a whole 4x4x16 slice. The times are simulated.
512 devices in a mesh: blk: 32 (over x, z_lo), col: 16 (over z_hi, y, core).
Axes of the slice: x: 4, y: 4, z: 16 (z_hi: 2, z_lo: 8; z = z_hi * 8 + z_lo), core: 2. Of those that a mesh axis runs over, the one named last changes fastest.
Arguments:
- probes: bfloat16 [8, 8, 32, 512], P(None, None, 'blk'), may hold values from -6 to 6
- diag_tiles: bfloat16 [8, 32, 512, 512], P(None, 'blk', 'col'), may hold values from -0.25 to 0.25
- left_factors: bfloat16 [8, 32, 2, 32, 32, 512], P(None, 'blk', None, 'col'), may hold values from -0.09375 to 0.09375
- right_factors: bfloat16 [8, 32, 2, 32, 32, 512], P(None, 'blk', None, 'col'), may hold values from -0.25 to 0.25
- ranks: int32 [8, 32, 2, 32], P(None, 'blk', None, 'col'), may hold values from 8 to 32
- present: int32 [8, 32, 2, 32], P(None, 'blk', None, 'col'), may hold values from 0 to 1, as said below
Outputs:
- product: float32 [8, 8, 32, 512], P(None, None, 'blk')
Inputs may be any that keep to these rules, and one draw needn't show every extreme that they name: A tile (i, i - d) is present exactly when i - d >= 0 and d is at most the band length of block row i; band lengths lie between 16 and 64, and some row's is 64.
All inputs are finite; a program needn't handle non-finite values.
Results may differ from a plain program's by a relative error of at most 0.0016.
Values may be sent and summed in bfloat16 or wider, within the bound.
A program may use at most 64 MiB of HBM per device.

v0:
```python
import jax
import jax.numpy as jnp
from jax import lax
from jax.sharding import PartitionSpec as P


def shifted(block, axis, distance):
    devices = range(lax.axis_size(axis))
    route = [((i - distance) % len(devices), i) for i in devices]
    return lax.ppermute(block, axis, route)


def drop_rows(values, amount):
    height = values.shape[1]
    if amount == 0:
        return values
    filler = jnp.zeros((values.shape[0], amount, values.shape[2]), values.dtype)
    return jnp.concatenate([filler, values[:, : height - amount]], 1)


def raise_rows(values, amount):
    height = values.shape[1]
    if amount == 0:
        return values
    filler = jnp.zeros((values.shape[0], amount, values.shape[2]), values.dtype)
    return jnp.concatenate([values[:, amount:], filler], 1)


def shards(probes, diag_tiles, left_factors, right_factors, ranks, present):
    own_probes = probes[:, :, 0, :]
    col_count = lax.axis_size("col")
    blk_index = lax.axis_index("blk")
    col_index = lax.axis_index("col")
    section_count = left_factors.shape[3]
    group_count = left_factors.shape[2]
    rank_cap = left_factors.shape[4]
    digit_count = (col_count - 1).bit_length()
    keep = (
        (jnp.arange(rank_cap)[None, None, None, :] < ranks[:, 0, :, :, None])
        & (present[:, 0, :, :, None] == 1)
    ).astype(jnp.float32)
    moving = shifted(own_probes, "blk", 1)
    for bit_pos in range(digit_count):
        farther = shifted(moving, "blk", section_count * (1 << bit_pos))
        moving = jnp.where(col_index >> bit_pos & 1 == 1, farther, moving)
    row_part = jnp.zeros(own_probes.shape, jnp.float32)
    carried = jnp.zeros(own_probes.shape, jnp.float32)
    for section_no in range(section_count):
        crossed = blk_index - 1 - col_index * section_count - section_no < 0
        for group_no in range(group_count):
            aligned = jnp.where(
                crossed, drop_rows(moving, group_no + 1), drop_rows(moving, group_no)
            )
            left_tile = left_factors[:, 0, group_no, section_no]
            right_tile = right_factors[:, 0, group_no, section_no]
            keep_here = keep[:, group_no, section_no][:, :, None]
            coeffs = (
                jnp.einsum("rkb,prb->rkp", right_tile, aligned, preferred_element_type=jnp.float32)
                * keep_here
            ).astype(jnp.bfloat16)
            row_part = row_part + jnp.einsum(
                "rkp,rkb->prb", coeffs, left_tile, preferred_element_type=jnp.float32
            )
            reverse_coef = (
                jnp.einsum(
                    "rkb,prb->rkp", left_tile, own_probes, preferred_element_type=jnp.float32
                )
                * keep_here
            ).astype(jnp.bfloat16)
            image_rows = jnp.einsum(
                "rkp,rkb->prb", reverse_coef, right_tile, preferred_element_type=jnp.float32
            )
            carried = carried + jnp.where(
                crossed, raise_rows(image_rows, group_no + 1), raise_rows(image_rows, group_no)
            )
        if section_no + 1 < section_count:
            moving = shifted(moving, "blk", 1)
            carried = shifted(carried, "blk", 1)
    for bit_pos in range(digit_count + 1):
        farther = shifted(carried, "blk", -section_count * (1 << bit_pos))
        carried = jnp.where(col_index + 1 >> bit_pos & 1 == 1, farther, carried)
    rows_here = diag_tiles.shape[2]
    diag_rows = jnp.einsum(
        "rab,prb->pra", diag_tiles[:, 0], own_probes, preferred_element_type=jnp.float32
    )
    placed = lax.dynamic_update_slice_in_dim(
        jnp.zeros(own_probes.shape, jnp.float32), diag_rows, col_index * rows_here, 2
    )
    combined = row_part + carried + placed
    summed = lax.psum(combined, "col")
    return summed[:, :, None, :]


def solution(mesh):
    return jax.shard_map(
        shards,
        mesh=mesh,
        in_specs=(
            P(None, None, "blk", None),
            P(None, "blk", "col", None),
            P(None, "blk", None, "col", None, None),
            P(None, "blk", None, "col", None, None),
            P(None, "blk", None, "col"),
            P(None, "blk", None, "col"),
        ),
        out_specs=P(None, None, "blk", None),
        check_vma=False,
    )
```

profile of v0, /device:TPU:1, one launch (start us, length us, event | category | flops | bytes accessed | tf_op | source)
XLA Modules:
  0.0 361.2 jit_solution(4883090299686959231)
XLA Ops:
  6.5 1.0 copy.37
  7.5 4.4 %collective-permute-start = (bf16[8,8,512]{2,0,1:T(8,128)(2,1)S(1)}, bf16[8,8,512]{2,0,1:T(8,128)(2,1)S(1)}, u32[]{:S(2)}, u32[]{:S(2)}) collective-permute-start(bf16[8,8,512]{2,0,1:T(8,128)(2,1)S(1)} %bitcast.114), channel_id=1, source_target_pairs={{496,0},{0,16},{16,32},{32,48},{48,64},{64,80},{80,96},{96,112},{1... | collective-permute-start | bytes 196616 | tf_op jit(solution)/shard_map/ppermute | solution.py:10
  11.9 0.7 compare_bitcast_fusion
  12.6 0.8 fusion.97
  13.4 0.0 copy-done.3
  13.4 1.3 convolution_bitcast_fusion.2
  14.7 0.0 copy-start.2
  14.7 0.7 copy-done.6
  15.4 1.2 convolution_bitcast_fusion.3
  16.7 0.9 slice-done.3
  17.6 3.5 collective-permute-start.6
  21.1 4.0 %collective-permute-done = bf16[8,8,512]{2,0,1:T(8,128)(2,1)S(1)} collective-permute-done((bf16[8,8,512]{2,0,1:T(8,128)(2,1)S(1)}, bf16[8,8,512]{2,0,1:T(8,128)(2,1)S(1)}, u32[]{:S(2)}, u32[]{:S(2)}) %collective-permute-start) | collective-permute-done | bytes 65568 | tf_op jit(solution)/shard_map/ppermute | solution.py:10
  25.1 2.2 collective-permute-start.1
  27.3 0.3 convolution_bitcast_fusion.1
  27.5 11.0 %collective-permute-done.1 = bf16[8,8,512]{2,0,1:T(8,128)(2,1)S(1)} collective-permute-done((bf16[8,8,512]{2,0,1:T(8,128)(2,1)S(1)}, bf16[8,8,512]{2,0,1:T(8,128)(2,1)S(1)}, u32[]{:S(2)}, u32[]{:S(2)}) %collective-permute-start.1) | collective-permute-done | bytes 65568 | tf_op jit(solution)/shard_map/ppermute | solution.py:10
  38.6 1.9 collective-permute-start.2
  40.5 0.3 convolution_bitcast_fusion
  40.8 0.7 copy-done.5
  41.5 8.1 %collective-permute-done.2 = bf16[8,8,512]{2,0,1:T(8,128)(2,1)S(1)} collective-permute-done((bf16[8,8,512]{2,0,1:T(8,128)(2,1)S(1)}, bf16[8,8,512]{2,0,1:T(8,128)(2,1)S(1)}, u32[]{:S(2)}, u32[]{:S(2)}) %collective-permute-start.2) | collective-permute-done | bytes 65568 | tf_op jit(solution)/shard_map/ppermute | solution.py:10
  49.6 1.9 collective-permute-start.3
  51.6 0.0 collective-permute-done.6
  51.6 0.1 select_add_fusion
  51.7 1.9 collective-permute-start.7
  53.6 2.4 collective-permute-done.3
  56.0 1.9 collective-permute-start.4
  57.9 2.0 collective-permute-done.7
  59.9 1.9 collective-permute-start.8
  61.9 0.7 collective-permute-done.4
  62.6 1.9 collective-permute-start.5
  64.6 6.6 %collective-permute-done.8 = f32[8,8,512]{2,0,1:T(8,128)S(1)} collective-permute-done((f32[8,8,512]{2,0,1:T(8,128)S(1)}, f32[8,8,512]{2,0,1:T(8,128)S(1)}, u32[]{:S(2)}, u32[]{:S(2)}) %collective-permute-start.8) | collective-permute-done | bytes 131104 | tf_op jit(solution)/shard_map/ppermute | solution.py:10
  71.1 4.2 %collective-permute-start.9 = (f32[8,8,512]{2,0,1:T(8,128)S(1)}, f32[8,8,512]{2,0,1:T(8,128)S(1)}, u32[]{:S(2)}, u32[]{:S(2)}) collective-permute-start(f32[8,8,512]{2,0,1:T(8,128)S(1)} %broadcast_select_fusion.1), channel_id=1, source_target_pairs={{128,0},{144,16},{160,32},{176,48},{192,64},{208,80},{224,96},{240... | collective-permute-start | bytes 393224 | tf_op jit(solution)/shard_map/ppermute | solution.py:10
  75.4 0.3 fusion.10
  75.7 2.9 collective-permute-done.9
  78.6 6.2 %collective-permute-start.10 = (f32[8,8,512]{2,0,1:T(8,128)S(1)}, f32[8,8,512]{2,0,1:T(8,128)S(1)}, u32[]{:S(2)}, u32[]{:S(2)}) collective-permute-start(f32[8,8,512]{2,0,1:T(8,128)S(1)} %broadcast_select_fusion.2), channel_id=1, source_target_pairs={{256,0},{272,16},{288,32},{304,48},{320,64},{336,80},{352,96},{368... | collective-permute-start | bytes 393224 | tf_op jit(solution)/shard_map/ppermute | solution.py:10
  84.8 0.3 convolution_add_fusion.2
  85.0 0.0 collective-permute-done.5
  85.1 2.1 collective-permute-done.10
  87.3 0.0 collective-permute-start.11
  87.3 0.3 convolution_add_fusion.1
  87.6 0.0 collective-permute-done.11
  87.6 0.3 fusion.9
  87.9 0.2 add_bitcast_fusion
  88.1 1.4 add.78
  89.4 0.0 copy-start.7
  89.4 0.6 copy-done.7
  90.1 0.0 all-reduce.12.cloned.1.call-update
  90.1 262.5 %all-reduce.12.cloned.1.call-done = f32[8,8,1,512]{3,0,1,2:T(8,128)} async-done(((f32[8,8,1,512]{3,0,1,2:T(8,128)}), f32[8,8,1,512]{3,0,1,2:T(8,128)}) %all-reduce.12.cloned.1.call-update) | async-done | bytes 131088 | tf_op jit(solution)/shard_map/psum | solution.py:90
  352.6 1.7 copy.16
  (34 shorter events, 0.2 us)
Async XLA Ops:
  6.5 81.3 %copy-start = (bf16[8,1,32,512]{3,2,1,0:T(8,128)(2,1)S(1)}, bf16[8,1,32,512]{3,2,1,0:T(8,128)(2,1)}, u32[]{:S(2)}) copy-start(bf16[8,1,32,512]{3,2,1,0:T(8,128)(2,1)} %param.7) | copy-start | bytes 786436
  6.5 6.8 %copy-start.3 = (bf16[8,8,1,512]{3,1,2,0:T(8,128)(2,1)S(1)}, bf16[8,8,1,512]{3,1,2,0:T(8,128)(2,1)}, u32[]{:S(2)}) copy-start(bf16[8,8,1,512]{3,1,2,0:T(8,128)(2,1)} %param.6) | copy-start | bytes 196612
  6.5 8.8 %copy-start.1 = (bf16[8,1,2,2,32,512]{5,4,3,2,1,0:T(8,128)(2,1)S(1)}, bf16[8,1,2,2,32,512]{5,4,3,2,1,0:T(8,128)(2,1)}, u32[]{:S(2)}) copy-start(bf16[8,1,2,2,32,512]{5,4,3,2,1,0:T(8,128)(2,1)} %param.8) | copy-start | bytes 3145732
  6.5 346.1 %all-reduce.12.cloned.1.call-start = ((), (), s32[]{:S(2)}) async-start(), calls=%async_computation | async-start | bytes 262144 | tf_op jit(solution)/shard_map/psum | solution.py:90
  7.5 17.6 %collective-permute-start = (bf16[8,8,512]{2,0,1:T(8,128)(2,1)S(1)}, bf16[8,8,512]{2,0,1:T(8,128)(2,1)S(1)}, u32[]{:S(2)}, u32[]{:S(2)}) collective-permute-start(bf16[8,8,512]{2,0,1:T(8,128)(2,1)S(1)} %bitcast.114), channel_id=1, source_target_pairs={{496,0},{0,16},{16,32},{32,48},{48,64},{64,80},{80,96},{96,112},{1... | collective-permute-start | bytes 196616 | tf_op jit(solution)/shard_map/ppermute | solution.py:10
  14.7 0.7 copy-start.6
  14.7 12.6 %copy-start.2 = (bf16[8,1,2,2,32,512]{5,4,3,2,1,0:T(8,128)(2,1)S(1)}, bf16[8,1,2,2,32,512]{5,4,3,2,1,0:T(8,128)(2,1)}, u32[]{:S(2)}) copy-start(bf16[8,1,2,2,32,512]{5,4,3,2,1,0:T(8,128)(2,1)} %param.9) | copy-start | bytes 3145732
  16.6 0.9 slice-start.3
  17.6 34.0 %collective-permute-start.6 = (f32[8,8,512]{2,0,1:T(8,128)S(1)}, f32[8,8,512]{2,0,1:T(8,128)S(1)}, u32[]{:S(2)}, u32[]{:S(2)}) collective-permute-start(f32[8,8,512]{2,0,1:T(8,128)S(1)} %select_add_fusion.1), channel_id=1, source_target_pairs={{496,0},{0,16},{16,32},{32,48},{48,64},{64,80},{80,96},{96,112},{1... | collective-permute-start | bytes 393224 | tf_op jit(solution)/shard_map/ppermute | solution.py:10
  25.1 13.5 %collective-permute-start.1 = (bf16[8,8,512]{2,0,1:T(8,128)(2,1)S(1)}, bf16[8,8,512]{2,0,1:T(8,128)(2,1)S(1)}, u32[]{:S(2)}, u32[]{:S(2)}) collective-permute-start(bf16[8,8,512]{2,0,1:T(8,128)(2,1)S(1)} %collective-permute-done), channel_id=1, source_target_pairs={{480,0},{496,16},{0,32},{16,48},{32,64},{48,80},{64,96},{80,112},{... | collective-permute-start | bytes 196616 | tf_op jit(solution)/shard_map/ppermute | solution.py:10
  27.5 13.9 %copy-start.4 = (f32[8,8,512]{2,0,1:T(8,128)}, f32[8,8,512]{2,0,1:T(8,128)S(1)}, u32[]{:S(2)}) copy-start(f32[8,8,512]{2,0,1:T(8,128)S(1)} %convolution_bitcast_fusion.1) | copy-start | bytes 393220
  38.6 11.0 %collective-permute-start.2 = (bf16[8,8,512]{2,0,1:T(8,128)(2,1)S(1)}, bf16[8,8,512]{2,0,1:T(8,128)(2,1)S(1)}, u32[]{:S(2)}, u32[]{:S(2)}) collective-permute-start(bf16[8,8,512]{2,0,1:T(8,128)(2,1)S(1)} %broadcast_select_fusion.4), channel_id=1, source_target_pairs={{448,0},{464,16},{480,32},{496,48},{0,64},{16,80},{32,96},{48,112}... | collective-permute-start | bytes 196616 | tf_op jit(solution)/shard_map/ppermute | solution.py:10
  40.8 0.7 copy-start.5
  41.5 10.1 %slice-start.2 = ((f32[8,8,512]{2,0,1:T(8,128)}), f32[8,6,512]{2,0,1:T(8,128)S(1)}, s32[]{:S(2)}) async-start(f32[8,8,512]{2,0,1:T(8,128)} %copy-done.5), calls=%async_computation.3 | async-start | bytes 196608 | tf_op jit(solution)/shard_map/slice | solution.py:26
  41.5 10.1 %slice-start = ((f32[8,8,512]{2,0,1:T(8,128)}), f32[8,7,512]{2,0,1:T(8,128)S(1)}, s32[]{:S(2)}) async-start(f32[8,8,512]{2,0,1:T(8,128)} %copy-done.4), calls=%async_computation.1 | async-start | bytes 229376 | tf_op jit(solution)/shard_map/slice | solution.py:26
  41.5 10.1 %slice-start.1 = ((f32[8,8,512]{2,0,1:T(8,128)}), f32[8,7,512]{2,0,1:T(8,128)S(1)}, s32[]{:S(2)}) async-start(f32[8,8,512]{2,0,1:T(8,128)} %copy-done.5), calls=%async_computation.2 | async-start | bytes 229376 | tf_op jit(solution)/shard_map/slice | solution.py:26
  49.6 6.4 %collective-permute-start.3 = (bf16[8,8,512]{2,0,1:T(8,128)(2,1)S(1)}, bf16[8,8,512]{2,0,1:T(8,128)(2,1)S(1)}, u32[]{:S(2)}, u32[]{:S(2)}) collective-permute-start(bf16[8,8,512]{2,0,1:T(8,128)(2,1)S(1)} %broadcast_select_fusion.5), channel_id=1, source_target_pairs={{384,0},{400,16},{416,32},{432,48},{448,64},{464,80},{480,96},{496... | collective-permute-start | bytes 196616 | tf_op jit(solution)/shard_map/ppermute | solution.py:10
  51.7 8.2 %collective-permute-start.7 = (f32[8,8,512]{2,0,1:T(8,128)S(1)}, f32[8,8,512]{2,0,1:T(8,128)S(1)}, u32[]{:S(2)}, u32[]{:S(2)}) collective-permute-start(f32[8,8,512]{2,0,1:T(8,128)S(1)} %select_add_fusion), channel_id=1, source_target_pairs={{32,0},{48,16},{64,32},{80,48},{96,64},{112,80},{128,96},{144,112}... | collective-permute-start | bytes 393224 | tf_op jit(solution)/shard_map/ppermute | solution.py:10
  56.0 6.6 %collective-permute-start.4 = (bf16[8,8,512]{2,0,1:T(8,128)(2,1)S(1)}, bf16[8,8,512]{2,0,1:T(8,128)(2,1)S(1)}, u32[]{:S(2)}, u32[]{:S(2)}) collective-permute-start(bf16[8,8,512]{2,0,1:T(8,128)(2,1)S(1)} %broadcast_select_fusion.6), channel_id=1, source_target_pairs={{256,0},{272,16},{288,32},{304,48},{320,64},{336,80},{352,96},{368... | collective-permute-start | bytes 196616 | tf_op jit(solution)/shard_map/ppermute | solution.py:10
  59.9 11.2 %collective-permute-start.8 = (f32[8,8,512]{2,0,1:T(8,128)S(1)}, f32[8,8,512]{2,0,1:T(8,128)S(1)}, u32[]{:S(2)}, u32[]{:S(2)}) collective-permute-start(f32[8,8,512]{2,0,1:T(8,128)S(1)} %broadcast_select_fusion), channel_id=1, source_target_pairs={{64,0},{80,16},{96,32},{112,48},{128,64},{144,80},{160,96},{176,11... | collective-permute-start | bytes 393224 | tf_op jit(solution)/shard_map/ppermute | solution.py:10
  62.6 22.4 %collective-permute-start.5 = (bf16[8,8,512]{2,0,1:T(8,128)(2,1)S(1)}, bf16[8,8,512]{2,0,1:T(8,128)(2,1)S(1)}, u32[]{:S(2)}, u32[]{:S(2)}) collective-permute-start(bf16[8,8,512]{2,0,1:T(8,128)(2,1)S(1)} %broadcast_select_fusion.7), channel_id=1, source_target_pairs={{496,0},{0,16},{16,32},{32,48},{48,64},{64,80},{80,96},{96,112},{1... | collective-permute-start | bytes 196616 | tf_op jit(solution)/shard_map/ppermute | solution.py:10
  71.1 7.4 %collective-permute-start.9 = (f32[8,8,512]{2,0,1:T(8,128)S(1)}, f32[8,8,512]{2,0,1:T(8,128)S(1)}, u32[]{:S(2)}, u32[]{:S(2)}) collective-permute-start(f32[8,8,512]{2,0,1:T(8,128)S(1)} %broadcast_select_fusion.1), channel_id=1, source_target_pairs={{128,0},{144,16},{160,32},{176,48},{192,64},{208,80},{224,96},{240... | collective-permute-start | bytes 393224 | tf_op jit(solution)/shard_map/ppermute | solution.py:10
  78.6 8.7 %collective-permute-start.10 = (f32[8,8,512]{2,0,1:T(8,128)S(1)}, f32[8,8,512]{2,0,1:T(8,128)S(1)}, u32[]{:S(2)}, u32[]{:S(2)}) collective-permute-start(f32[8,8,512]{2,0,1:T(8,128)S(1)} %broadcast_select_fusion.2), channel_id=1, source_target_pairs={{256,0},{272,16},{288,32},{304,48},{320,64},{336,80},{352,96},{368... | collective-permute-start | bytes 393224 | tf_op jit(solution)/shard_map/ppermute | solution.py:10
  87.3 0.3 collective-permute-start.11
  89.4 0.7 copy-start.7
Sparse Core Ops, SparseCore 0:
  90.2 262.3 all-reduce.11
where the time goes:
time: 362 us; the launch traced here: 361 us
  waiting for transfers between devices  302 us (83%)
  starting transfers between devices  32 us (9%)
  between operations  13.7 us (4%)
  local copies, waits for them, and re-layouts  6.96 us (2%)
  matrix products  4.47 us (1%)
    psum x1, waiting for transfers between devices, shards(): summed = lax.psum(combined, 'col')  263 us
    ppermute x12, waiting for transfers between devices, shifted(): return lax.ppermute(block, axis, route)  39.8 us
    ppermute x12, starting transfers between devices, shifted(): return lax.ppermute(block, axis, route)  32 us
  transfers between devices with their start and end apart: 13, of which 10 were waited for; matrix products, arithmetic and copies ran while one was open for 2% of the time, Pallas kernels for 0%

commit v1 on v0

v1 whole, which is shorter than its diff:
```python
import functools

import jax
import jax.numpy as jnp
from jax import lax
from jax.experimental import pallas as pl
from jax.experimental.pallas import tpu as pltpu
from jax.sharding import PartitionSpec as P

MESH = pl.DeviceIdType.MESH
BF16 = jnp.bfloat16
F32 = jnp.float32

NBLK = 32
HALF = 8
ZRING = 16
ZLOW = 8


def dot(a, b):
    return lax.dot_general(a, b, (((1,), (0,)), ((), ())), preferred_element_type=F32)


def dot_t(a, b):
    return lax.dot_general(a, b, (((1,), (1,)), ((), ())), preferred_element_type=F32)


def partners(b, c, s):
    zl = lax.rem(b, ZLOW)
    zh = lax.div(c, HALF)
    g = lax.rem(c, HALF)
    z = zh * ZLOW + zl
    flip = g if s == 0 else g + 1 - 2 * lax.rem(g, 2)
    src_b = lax.rem(b + 2 * NBLK - (2 * c + 1 + s), NBLK)
    src_h = lax.rem(lax.div(z - lax.rem(src_b, ZLOW) + ZRING + 4, ZLOW), 2)
    shift = 2 * flip + 1 + s
    dst_h = lax.rem(lax.div(lax.rem(zl + shift, ZLOW) - z + ZRING + 4, ZLOW), 2)
    dst_b = lax.rem(b + shift + 16 * dst_h, NBLK)
    return (src_b, src_h * HALF + flip), (dst_b, dst_h * HALF + flip)


def quarter(b, c, up):
    zl = lax.rem(b, ZLOW)
    z = lax.rem(lax.div(c, HALF) * ZLOW + zl + up, ZRING)
    return b - zl + lax.rem(z, ZLOW), lax.div(z, ZLOW) * HALF + lax.rem(c, HALF)


def kernel(
    x_hbm, d_hbm, u_hbm, v_hbm, rank_hbm, pres_hbm, out,
    x_v, d_v, u_v, v_v, rank_v, pres_v, y_v, car_out, car_in, rs_out, rs_in, zx_out, zx_in,
    in_sem, y_ssem, y_rsem, car_ssem, car_rsem, rs_ssem, rs_rsem, zx_ssem, zx_rsem, ag_ssem, ag_rsem, met_sem,
):
    def load(i, src, dst):
        copy = pltpu.make_async_copy(src, dst, in_sem.at[i])
        copy.start()
        return copy

    small = [load(0, rank_hbm, rank_v), load(1, pres_hbm, pres_v)]
    x_load = load(2, x_hbm, x_v)
    tiles = [
        [load(3 + 2 * s, u_hbm.at[:, :, s], u_v.at[:, :, s]), load(4 + 2 * s, v_hbm.at[:, :, s], v_v.at[:, :, s])]
        for s in range(2)
    ]
    d_load = load(7, d_hbm, d_v)

    b = lax.axis_index("blk")
    c = lax.axis_index("col")
    pairs = [partners(b, c, s) for s in range(2)]
    g = lax.rem(c, HALF)
    base = c - g
    far_first = (4, 5, 3, 2, 6, 7, 1)
    ids = [lax.rem(g + o, HALF) for o in far_first]
    group = [(b, base + i) for i in ids]
    across = (b, lax.rem(c + HALF, 2 * HALF))
    above, below = quarter(b, c, 4), quarter(b, c, 12)

    barrier = pltpu.get_barrier_semaphore()
    peers = [pairs[0][0], pairs[1][0], pairs[0][1], pairs[1][1], above, below] + group
    for peer in peers:
        pl.semaphore_signal(barrier, inc=1, device_id=peer, device_id_type=MESH)

    def remote(src, dst, ssem, rsem, device):
        return pltpu.make_async_remote_copy(
            src_ref=src, dst_ref=dst, send_sem=ssem, recv_sem=rsem, device_id=device, device_id_type=MESH
        )

    def wait_bytes(ref, sem):
        pltpu.make_async_copy(ref, ref, sem).wait()

    y_copies = [remote(x_hbm, y_v.at[s], y_ssem.at[s], y_rsem.at[s], pairs[s][1]) for s in range(2)]
    pl.semaphore_wait(barrier, len(peers))
    for copy in y_copies:
        copy.start()
    pl.semaphore_signal(met_sem, inc=1, device_id=below, device_id_type=MESH)

    for copy in small:
        copy.wait()
    lane = lax.broadcasted_iota(jnp.int32, (8, 512), 1)
    row = lax.broadcasted_iota(jnp.int32, (8, 512), 0)
    lane_r = lane >> 6
    lane_q = (lane >> 5) & 1
    lane_k = (lane & 31).astype(F32)
    spread = (row == lane_r).astype(BF16)
    height = [dot((rank_v[q] * pres_v[q]).astype(F32).astype(BF16), spread) for q in range(2)]
    kept, shift = [], []
    for s in range(2):
        kept.append(lane_k < jnp.where(lane_q == 0, height[0][s : s + 1], height[1][s : s + 1]))
        shift.append(lane_q + jnp.where(b < 2 * c + 1 + s, 1, 0))

    def pick(a, step, s, rows):
        a = a.reshape(8, 8, 512)
        once, twice = pltpu.roll(a, step % 8, 1), pltpu.roll(a, 2 * step % 8, 1)
        a = jnp.where(shift[s][None] == 0, a, jnp.where(shift[s][None] == 1, once, twice))
        return jnp.where((kept[s] & (lane_r == rows))[None], a, 0.0).reshape(64, 512).astype(BF16)

    def section(ref, s):
        return ref[:, :, s].reshape(512, 512)

    x_load.wait()
    x = x_v[...]
    car_copies = []
    for s in range(2):
        tiles[s][0].wait()
        t = pick(dot_t(x, section(u_v, s)), -1, s, row + shift[s])
        tiles[s][1].wait()
        car_out[s] = dot(t, section(v_v, s)).astype(BF16)
        copy = remote(car_out.at[s], car_in.at[s], car_ssem.at[s], car_rsem.at[s], pairs[s][0])
        copy.start()
        car_copies.append(copy)

    d_load.wait()
    dg = dot_t(x, d_v[...]).reshape(8, 8, 256)
    dg = jnp.where((lane[:, :256] >> 5 == row[:, :256])[None], dg, 0.0).reshape(64, 256)
    dg = dg[:, :128] + dg[:, 128:]
    dg = dg + pltpu.roll(dg, 64, 1)
    dg = dg + pltpu.roll(dg, 32, 1)
    total = jnp.concatenate([dg] * 4, 1).reshape(8, 8, 512)
    total = jnp.where((lane >> 5 == c)[None], total, 0.0).reshape(64, 512)

    for s in range(2):
        y_copies[s].wait_recv()
        a = pick(dot_t(y_v[s], section(v_v, s)), 1, s, row)
        total = total + dot(a, section(u_v, s))
    for s in range(2):
        car_copies[s].wait_recv()
        total = total + car_in[s].astype(F32)

    rs_out[...] = total.reshape(8, 8, 512)
    for i, peer in zip(ids, group):
        remote(rs_out.at[i], rs_in.at[g], rs_ssem, rs_rsem, peer).start()
    rs_in[g] = rs_out[g]
    for copy in y_copies + car_copies:
        copy.wait_send()
    wait_bytes(rs_in.at[pl.ds(0, HALF - 1)], rs_rsem)
    part = rs_in[0]
    for p in range(1, HALF):
        part = part + rs_in[p]

    zx_out[...] = part
    zx_copy = remote(zx_out, zx_in, zx_ssem, zx_rsem, across)
    pl.semaphore_wait(met_sem, 1)
    zx_copy.start()
    wait_bytes(rs_out.at[pl.ds(0, HALF - 1)], rs_ssem)
    zx_copy.wait_recv()
    whole = part + zx_in[...]
    for k in range(4):
        out[pl.ds(32 * g + k, 8, stride=4), :] = whole[:, 128 * k : 128 * k + 128]

    mine = out.at[pl.ds(pl.multiple_of(32 * g, 32), 32)]
    for peer in group:
        remote(mine, mine, ag_ssem, ag_rsem, peer).start()
    zx_copy.wait_send()
    others = out.at[pl.ds(0, 32 * (HALF - 1))]
    wait_bytes(others, ag_rsem)
    wait_bytes(others, ag_ssem)


def shards(probes, diag_tiles, left_factors, right_factors, ranks, present):
    hbm = pl.BlockSpec(memory_space=pltpu.HBM)
    dma = pltpu.SemaphoreType.DMA
    out = pl.pallas_call(
        kernel,
        out_shape=pltpu.VMEM((256, 128), F32),
        in_specs=[hbm] * 6,
        out_specs=pl.BlockSpec(memory_space=pltpu.VMEM),
        scratch_shapes=[
            pltpu.VMEM((64, 512), BF16),
            pltpu.VMEM((256, 512), BF16),
            pltpu.VMEM((8, 2, 2, 32, 512), BF16),
            pltpu.VMEM((8, 2, 2, 32, 512), BF16),
            pltpu.VMEM((2, 2, 8), jnp.int32),
            pltpu.VMEM((2, 2, 8), jnp.int32),
            pltpu.VMEM((2, 64, 512), BF16),
            pltpu.VMEM((2, 64, 512), BF16),
            pltpu.VMEM((2, 64, 512), BF16),
            pltpu.VMEM((8, 8, 512), F32),
            pltpu.VMEM((8, 8, 512), F32),
            pltpu.VMEM((8, 512), F32),
            pltpu.VMEM((8, 512), F32),
            dma((8,)),
            dma((2,)),
            dma((2,)),
            dma((2,)),
            dma((2,)),
            dma,
            dma,
            dma,
            dma,
            dma,
            dma,
            pltpu.SemaphoreType.REGULAR,
        ],
        compiler_params=pltpu.CompilerParams(
            collective_id=0, has_side_effects=True, vmem_limit_bytes=60 * 1024 * 1024
        ),
        cost_estimate=pl.CostEstimate(flops=300_000_000, bytes_accessed=2_500_000, transcendentals=0),
    )(
        probes.reshape(64, 512),
        diag_tiles.reshape(256, 512),
        left_factors[:, 0],
        right_factors[:, 0],
        jnp.transpose(ranks[:, 0], (1, 2, 0)),
        jnp.transpose(present[:, 0], (1, 2, 0)),
    )
    return out.reshape(8, 8, 1, 512)


def solution(mesh):
    return jax.shard_map(
        shards,
        mesh=mesh,
        in_specs=(
            P(None, None, "blk", None),
            P(None, "blk", "col", None),
            P(None, "blk", None, "col", None, None),
            P(None, "blk", None, "col", None, None),
            P(None, "blk", None, "col"),
            P(None, "blk", None, "col"),
        ),
        out_specs=P(None, None, "blk", None),
        check_vma=False,
    )
```

time: 362 us -> 40.3 us (0.11)
  waiting for transfers between devices: 302 us -> 0 us
  Pallas kernels: 0 us -> 39.5 us
  starting transfers between devices: 32 us -> 0 us
  between operations: 13.7 us -> 0.01 us
  local copies, waits for them, and re-layouts: 6.96 us -> 0.66 us
  matrix products: 4.47 us -> 0 us
    psum x1 -> x0, waiting for transfers between devices: 263 us -> none  [shards(): summed = lax.psum(combined, 'col')]
    ppermute x12 -> x0, waiting for transfers between devices: 39.8 us -> none  [shifted(): return lax.ppermute(block, axis, route)]
    pallas_call x0 -> x1, Pallas kernels: none -> 39.5 us  [shards(): pl.pallas_call(kernel, out_shape=pltpu.VMEM((256, 128), F32), in_specs=[h...]
    ppermute x12 -> x0, starting transfers between devices: 32 us -> none  [shifted(): return lax.ppermute(block, axis, route)]
    dot_general x9 -> x0, matrix products: 4.47 us -> none  [the longest x4 3.14 us: shards(): jnp.einsum('rkp,rkb->prb', reverse_coef, right_tile, preferred_element_ty...]
  transfers between devices with their start and end apart: 13 -> 0, of which waited for: 10 -> 0; matrix products, arithmetic and copies ran while one was open for 2% -> 0% of each run, Pallas kernels for 0% -> 0%
where the time goes in v1:
time: 40.3 us; the launch traced here: 40.2 us
  Pallas kernels  39.5 us (98%)
  local copies, waits for them, and re-layouts  0.66 us (2%)
    pallas_call x1, Pallas kernels, shards(): pl.pallas_call(kernel, out_shape=pltpu.VMEM((256, 128), F32), in_specs=[h...  39.5 us

profile of v1, /device:TPU:1, one launch (start us, length us, event | category | flops | bytes accessed | tf_op | source)
XLA Modules:
  0.0 40.2 jit_solution(9388006519945227432)
XLA Ops:
  0.0 39.5 %shard_map.64 = f32[256,128]{1,0:T(8,128)S(1)} custom-call(bf16[64,512]{1,0:T(8,128)(2,1)} %bitcast.15, bf16[256,512]{1,0:T(8,128)(2,1)} %bitcast.14, bf16[8,2,2,32,512]{4,3,2,1,0:T(8,128)(2,1)} %bitcast.12, bf16[8,2,2,32,512]{4,3,2,1,0:T(8,128)(2,1)} %bitcast.13, s32[2,2,8]{2,1,0:T(2,128)} %bitcast.16, s32[2,2,8]{2,1,0:T(2,128)} %bitcast.17), custom_call_target="tpu_custom_call" | custom-call | flops 300000000 | bytes 2500000 | tf_op jit(solution)/shard_map/pallas_call | solution.py:181
  39.6 0.7 %copy.9 = f32[8,8,1,512]{3,2,1,0:T(1,128)} copy(f32[8,8,1,512]{3,2,1,0:T(1,128)S(1)} %bitcast.11) | data formatting | bytes 262144

commit v2 on v1

--- a/solution.py
+++ b/solution.py
@@ -50,34 +50,36 @@
     x_v, d_v, u_v, v_v, rank_v, pres_v, y_v, car_out, car_in, rs_out, rs_in, zx_out, zx_in,
     in_sem, y_ssem, y_rsem, car_ssem, car_rsem, rs_ssem, rs_rsem, zx_ssem, zx_rsem, ag_ssem, ag_rsem, met_sem,
 ):
+    b = lax.axis_index("blk")
+    c = lax.axis_index("col")
+    barrier = pltpu.get_barrier_semaphore()
+
+    def greet(peers):
+        for peer in peers:
+            pl.semaphore_signal(barrier, inc=1, device_id=peer, device_id_type=MESH)
+
     def load(i, src, dst):
         copy = pltpu.make_async_copy(src, dst, in_sem.at[i])
         copy.start()
         return copy
 
+    pairs = [partners(b, c, s) for s in range(2)]
+    greet([pairs[0][0], pairs[1][0], pairs[0][1], pairs[1][1]])
     small = [load(0, rank_hbm, rank_v), load(1, pres_hbm, pres_v)]
     x_load = load(2, x_hbm, x_v)
+    above, below = quarter(b, c, 4), quarter(b, c, 12)
+    g = lax.rem(c, HALF)
+    base = c - g
+    far_first = (4, 5, 3, 2, 6, 7, 1)
+    ids = [lax.rem(g + o, HALF) for o in far_first]
+    group = [(b, base + i) for i in ids]
+    greet([above, below] + group)
     tiles = [
         [load(3 + 2 * s, u_hbm.at[:, :, s], u_v.at[:, :, s]), load(4 + 2 * s, v_hbm.at[:, :, s], v_v.at[:, :, s])]
         for s in range(2)
     ]
     d_load = load(7, d_hbm, d_v)
-
-    b = lax.axis_index("blk")
-    c = lax.axis_index("col")
-    pairs = [partners(b, c, s) for s in range(2)]
-    g = lax.rem(c, HALF)
-    base = c - g
-    far_first = (4, 5, 3, 2, 6, 7, 1)
-    ids = [lax.rem(g + o, HALF) for o in far_first]
-    group = [(b, base + i) for i in ids]
     across = (b, lax.rem(c + HALF, 2 * HALF))
-    above, below = quarter(b, c, 4), quarter(b, c, 12)
-
-    barrier = pltpu.get_barrier_semaphore()
-    peers = [pairs[0][0], pairs[1][0], pairs[0][1], pairs[1][1], above, below] + group
-    for peer in peers:
-        pl.semaphore_signal(barrier, inc=1, device_id=peer, device_id_type=MESH)
 
     def remote(src, dst, ssem, rsem, device):
         return pltpu.make_async_remote_copy(
@@ -87,12 +89,7 @@
     def wait_bytes(ref, sem):
         pltpu.make_async_copy(ref, ref, sem).wait()
 
-    y_copies = [remote(x_hbm, y_v.at[s], y_ssem.at[s], y_rsem.at[s], pairs[s][1]) for s in range(2)]
-    pl.semaphore_wait(barrier, len(peers))
-    for copy in y_copies:
-        copy.start()
-    pl.semaphore_signal(met_sem, inc=1, device_id=below, device_id_type=MESH)
-
+    y_copies = [remote(x_v, y_v.at[s], y_ssem.at[s], y_rsem.at[s], pairs[s][1]) for s in range(2)]
     for copy in small:
         copy.wait()
     lane = lax.broadcasted_iota(jnp.int32, (8, 512), 1)
@@ -118,15 +115,19 @@
 
     x_load.wait()
     x = x_v[...]
-    car_copies = []
     for s in range(2):
         tiles[s][0].wait()
         t = pick(dot_t(x, section(u_v, s)), -1, s, row + shift[s])
         tiles[s][1].wait()
         car_out[s] = dot(t, section(v_v, s)).astype(BF16)
-        copy = remote(car_out.at[s], car_in.at[s], car_ssem.at[s], car_rsem.at[s], pairs[s][0])
+    car_copies = [
+        remote(car_out.at[s], car_in.at[s], car_ssem.at[s], car_rsem.at[s], pairs[s][0]) for s in range(2)
+    ]
+
+    pl.semaphore_wait(barrier, 6 + len(group))
+    for copy in y_copies + car_copies:
         copy.start()
-        car_copies.append(copy)
+    pl.semaphore_signal(met_sem, inc=1, device_id=below, device_id_type=MESH)
 
     d_load.wait()
     dg = dot_t(x, d_v[...]).reshape(8, 8, 256)

time: 40.3 us -> 39.7 us (0.985)
  Pallas kernels: 39.5 us -> 38.9 us
    pallas_call x1, Pallas kernels: 39.5 us -> 38.9 us  [shards(): pl.pallas_call(kernel, out_shape=pltpu.VMEM((256, 128), F32), in_specs=[h...]
where the time goes in v2:
time: 39.7 us; the launch traced here: 39.6 us
  Pallas kernels  38.9 us (98%)
  local copies, waits for them, and re-layouts  0.66 us (2%)
    pallas_call x1, Pallas kernels, shards(): pl.pallas_call(kernel, out_shape=pltpu.VMEM((256, 128), F32), in_specs=[h...  38.9 us

profile of v2, /device:TPU:1, one launch (start us, length us, event | category | flops | bytes accessed | tf_op | source)
XLA Modules:
  0.0 39.6 jit_solution(11075069984685354757)
XLA Ops:
  0.0 38.9 %shard_map.64 = f32[256,128]{1,0:T(8,128)S(1)} custom-call(bf16[64,512]{1,0:T(8,128)(2,1)} %bitcast.15, bf16[256,512]{1,0:T(8,128)(2,1)} %bitcast.14, bf16[8,2,2,32,512]{4,3,2,1,0:T(8,128)(2,1)} %bitcast.12, bf16[8,2,2,32,512]{4,3,2,1,0:T(8,128)(2,1)} %bitcast.13, s32[2,2,8]{2,1,0:T(2,128)} %bitcast.16, s32[2,2,8]{2,1,0:T(2,128)} %bitcast.17), custom_call_target="tpu_custom_call" | custom-call | flops 300000000 | bytes 2500000 | tf_op jit(solution)/shard_map/pallas_call | solution.py:182
  38.9 0.7 %copy.9 = f32[8,8,1,512]{3,2,1,0:T(1,128)} copy(f32[8,8,1,512]{3,2,1,0:T(1,128)S(1)} %bitcast.11) | data formatting | bytes 262144

commit v3 on v2

--- a/solution.py
+++ b/solution.py
@@ -15,6 +15,7 @@
 HALF = 8
 ZRING = 16
 ZLOW = 8
+CHUNK = 32
 
 
 def dot(a, b):
@@ -47,8 +48,8 @@
 
 def kernel(
     x_hbm, d_hbm, u_hbm, v_hbm, rank_hbm, pres_hbm, out,
-    x_v, d_v, u_v, v_v, rank_v, pres_v, y_v, car_out, car_in, rs_out, rs_in, zx_out, zx_in,
-    in_sem, y_ssem, y_rsem, car_ssem, car_rsem, rs_ssem, rs_rsem, zx_ssem, zx_rsem, ag_ssem, ag_rsem, met_sem,
+    x_v, d_v, u_v, v_v, rank_v, pres_v, y_v, car_tmp, car_out, car_in, rs_out, rs_in, zx_out, zx_in,
+    in_sem, y_ssem, y_rsem, car_ssem, car_rsem, rs_ssem, rs_rsem, zx_ssem, zx_rsem, ag_ssem, ag_rsem, met_sem, open_sem,
 ):
     b = lax.axis_index("blk")
     c = lax.axis_index("col")
@@ -119,14 +120,16 @@
         tiles[s][0].wait()
         t = pick(dot_t(x, section(u_v, s)), -1, s, row + shift[s])
         tiles[s][1].wait()
-        car_out[s] = dot(t, section(v_v, s)).astype(BF16)
-    car_copies = [
-        remote(car_out.at[s], car_in.at[s], car_ssem.at[s], car_rsem.at[s], pairs[s][0]) for s in range(2)
-    ]
+        image = dot(t, section(v_v, s))
+        for k in range(4):
+            car_tmp[s, pl.ds(k, 64, stride=4), :] = image[:, 128 * k : 128 * k + 128]
+        car_out[s] = car_tmp[s].reshape(HALF, CHUNK, 128).astype(BF16)
 
     pl.semaphore_wait(barrier, 6 + len(group))
-    for copy in y_copies + car_copies:
+    for copy in y_copies:
         copy.start()
+    for s in range(2):
+        pl.semaphore_signal(open_sem.at[s], inc=1, device_id=pairs[s][1], device_id_type=MESH)
     pl.semaphore_signal(met_sem, inc=1, device_id=below, device_id_type=MESH)
 
     d_load.wait()
@@ -138,40 +141,60 @@
     total = jnp.concatenate([dg] * 4, 1).reshape(8, 8, 512)
     total = jnp.where((lane >> 5 == c)[None], total, 0.0).reshape(64, 512)
 
+    at_home = c == 2 * HALF - 1
+    for s in range(2):
+        pl.semaphore_wait(open_sem.at[s], 1)
+        src_b, src_c = pairs[s][0]
+        src_base = src_c - lax.rem(src_c, HALF)
+        for i in ids + [g]:
+            src, dst = car_out.at[s, i], car_in.at[s, g]
+            copy = remote(src, dst, car_ssem, car_rsem, (src_b, src_base + i))
+            if s == 1 and i is g:
+                inside = pltpu.make_async_copy(src, dst, car_rsem)
+                pl.when(at_home)(lambda: inside.start())
+                pl.when(jnp.logical_not(at_home))(lambda: copy.start())
+            else:
+                copy.start()
+
     for s in range(2):
         y_copies[s].wait_recv()
         a = pick(dot_t(y_v[s], section(v_v, s)), 1, s, row)
         total = total + dot(a, section(u_v, s))
-    for s in range(2):
-        car_copies[s].wait_recv()
-        total = total + car_in[s].astype(F32)
-
-    rs_out[...] = total.reshape(8, 8, 512)
+    for k in range(4):
+        rs_out[pl.ds(k, 64, stride=4), :] = total[:, 128 * k : 128 * k + 128]
+
+    def chunk(i):
+        return pl.ds(pl.multiple_of(CHUNK * i, CHUNK), CHUNK)
+
     for i, peer in zip(ids, group):
-        remote(rs_out.at[i], rs_in.at[g], rs_ssem, rs_rsem, peer).start()
-    rs_in[g] = rs_out[g]
-    for copy in y_copies + car_copies:
+        remote(rs_out.at[chunk(i)], rs_in.at[g], rs_ssem, rs_rsem, peer).start()
+    rs_in[g] = rs_out[chunk(g), :]
+    for copy in y_copies:
         copy.wait_send()
+
+    wait_bytes(car_in, car_rsem)
+    part = car_in[0, 0].astype(F32)
+    for j in range(1, 2 * HALF):
+        part = part + car_in[j // HALF, j % HALF].astype(F32)
     wait_bytes(rs_in.at[pl.ds(0, HALF - 1)], rs_rsem)
-    part = rs_in[0]
-    for p in range(1, HALF):
-        part = part + rs_in[p]
-
+    for j in range(HALF):
+        part = part + rs_in[j]
     zx_out[...] = part
     zx_copy = remote(zx_out, zx_in, zx_ssem, zx_rsem, across)
     pl.semaphore_wait(met_sem, 1)
     zx_copy.start()
-    wait_bytes(rs_out.at[pl.ds(0, HALF - 1)], rs_ssem)
+    wait_bytes(rs_in.at[pl.ds(0, HALF - 1)], rs_ssem)
+    wait_bytes(car_out.at[0], car_ssem)
+    pl.when(at_home)(lambda: wait_bytes(car_out.at[1, pl.ds(0, HALF - 1)], car_ssem))
+    pl.when(jnp.logical_not(at_home))(lambda: wait_bytes(car_out.at[1], car_ssem))
+
     zx_copy.wait_recv()
-    whole = part + zx_in[...]
-    for k in range(4):
-        out[pl.ds(32 * g + k, 8, stride=4), :] = whole[:, 128 * k : 128 * k + 128]
-
-    mine = out.at[pl.ds(pl.multiple_of(32 * g, 32), 32)]
+    mine = out.at[chunk(g)]
+    mine[...] = part + zx_in[...]
     for peer in group:
         remote(mine, mine, ag_ssem, ag_rsem, peer).start()
     zx_copy.wait_send()
-    others = out.at[pl.ds(0, 32 * (HALF - 1))]
+    others = out.at[pl.ds(0, CHUNK * (HALF - 1))]
     wait_bytes(others, ag_rsem)
     wait_bytes(others, ag_ssem)
 
@@ -192,17 +215,18 @@
             pltpu.VMEM((2, 2, 8), jnp.int32),
             pltpu.VMEM((2, 2, 8), jnp.int32),
             pltpu.VMEM((2, 64, 512), BF16),
-            pltpu.VMEM((2, 64, 512), BF16),
-            pltpu.VMEM((2, 64, 512), BF16),
-            pltpu.VMEM((8, 8, 512), F32),
-            pltpu.VMEM((8, 8, 512), F32),
-            pltpu.VMEM((8, 512), F32),
-            pltpu.VMEM((8, 512), F32),
+            pltpu.VMEM((2, 256, 128), F32),
+            pltpu.VMEM((2, HALF, CHUNK, 128), BF16),
+            pltpu.VMEM((2, HALF, CHUNK, 128), BF16),
+            pltpu.VMEM((256, 128), F32),
+            pltpu.VMEM((HALF, CHUNK, 128), F32),
+            pltpu.VMEM((CHUNK, 128), F32),
+            pltpu.VMEM((CHUNK, 128), F32),
             dma((8,)),
             dma((2,)),
             dma((2,)),
-            dma((2,)),
-            dma((2,)),
+            dma,
+            dma,
             dma,
             dma,
             dma,
@@ -210,6 +234,7 @@
             dma,
             dma,
             pltpu.SemaphoreType.REGULAR,
+            pltpu.SemaphoreType.REGULAR((2,)),
         ],
         compiler_params=pltpu.CompilerParams(
             collective_id=0, has_side_effects=True, vmem_limit_bytes=60 * 1024 * 1024

time: 39.7 us -> 37.9 us (0.955)
  Pallas kernels: 38.9 us -> 37.1 us
    pallas_call x1, Pallas kernels: 38.9 us -> 37.1 us  [shards(): pl.pallas_call(kernel, out_shape=pltpu.VMEM((256, 128), F32), in_specs=[h...]
where the time goes in v3:
time: 37.9 us; the launch traced here: 37.8 us
  Pallas kernels  37.1 us (98%)
  local copies, waits for them, and re-layouts  0.66 us (2%)
    pallas_call x1, Pallas kernels, shards(): pl.pallas_call(kernel, out_shape=pltpu.VMEM((256, 128), F32), in_specs=[h...  37.1 us

profile of v3, /device:TPU:1, one launch (start us, length us, event | category | flops | bytes accessed | tf_op | source)
XLA Modules:
  0.0 37.8 jit_solution(12193001563343966985)
XLA Ops:
  0.0 37.1 %shard_map.64 = f32[256,128]{1,0:T(8,128)S(1)} custom-call(bf16[64,512]{1,0:T(8,128)(2,1)} %bitcast.15, bf16[256,512]{1,0:T(8,128)(2,1)} %bitcast.14, bf16[8,2,2,32,512]{4,3,2,1,0:T(8,128)(2,1)} %bitcast.12, bf16[8,2,2,32,512]{4,3,2,1,0:T(8,128)(2,1)} %bitcast.13, s32[2,2,8]{2,1,0:T(2,128)} %bitcast.16, s32[2,2,8]{2,1,0:T(2,128)} %bitcast.17), custom_call_target="tpu_custom_call" | custom-call | flops 300000000 | bytes 2500000 | tf_op jit(solution)/shard_map/pallas_call | solution.py:205
  37.1 0.7 %copy.9 = f32[8,8,1,512]{3,2,1,0:T(1,128)} copy(f32[8,8,1,512]{3,2,1,0:T(1,128)S(1)} %bitcast.11) | data formatting | bytes 262144

commit v4 on v3

--- a/solution.py
+++ b/solution.py
@@ -31,7 +31,7 @@
     zh = lax.div(c, HALF)
     g = lax.rem(c, HALF)
     z = zh * ZLOW + zl
-    flip = g if s == 0 else g + 1 - 2 * lax.rem(g, 2)
+    flip = g + lax.rem(g, 2) * (HALF - 2 * g)
     src_b = lax.rem(b + 2 * NBLK - (2 * c + 1 + s), NBLK)
     src_h = lax.rem(lax.div(z - lax.rem(src_b, ZLOW) + ZRING + 4, ZLOW), 2)
     shift = 2 * flip + 1 + s

time: 37.9 us -> 38.6 us (1.018)
  Pallas kernels: 37.1 us -> 37.8 us
    pallas_call x1, Pallas kernels: 37.1 us -> 37.8 us  [shards(): pl.pallas_call(kernel, out_shape=pltpu.VMEM((256, 128), F32), in_specs=[h...]
where the time goes in v4:
time: 38.6 us; the launch traced here: 38.5 us
  Pallas kernels  37.8 us (98%)
  local copies, waits for them, and re-layouts  0.66 us (2%)
    pallas_call x1, Pallas kernels, shards(): pl.pallas_call(kernel, out_shape=pltpu.VMEM((256, 128), F32), in_specs=[h...  37.8 us

profile of v4, /device:TPU:1, one launch (start us, length us, event | category | flops | bytes accessed | tf_op | source)
XLA Modules:
  0.0 38.5 jit_solution(16481586361790130761)
XLA Ops:
  0.0 37.8 %shard_map.64 = f32[256,128]{1,0:T(8,128)S(1)} custom-call(bf16[64,512]{1,0:T(8,128)(2,1)} %bitcast.15, bf16[256,512]{1,0:T(8,128)(2,1)} %bitcast.14, bf16[8,2,2,32,512]{4,3,2,1,0:T(8,128)(2,1)} %bitcast.12, bf16[8,2,2,32,512]{4,3,2,1,0:T(8,128)(2,1)} %bitcast.13, s32[2,2,8]{2,1,0:T(2,128)} %bitcast.16, s32[2,2,8]{2,1,0:T(2,128)} %bitcast.17), custom_call_target="tpu_custom_call" | custom-call | flops 300000000 | bytes 2500000 | tf_op jit(solution)/shard_map/pallas_call | solution.py:205
  37.8 0.7 %copy.9 = f32[8,8,1,512]{3,2,1,0:T(1,128)} copy(f32[8,8,1,512]{3,2,1,0:T(1,128)S(1)} %bitcast.11) | data formatting | bytes 262144

commit v5 on v3

--- a/solution.py
+++ b/solution.py
@@ -126,10 +126,10 @@
         car_out[s] = car_tmp[s].reshape(HALF, CHUNK, 128).astype(BF16)
 
     pl.semaphore_wait(barrier, 6 + len(group))
+    for s in range(2):
+        pl.semaphore_signal(open_sem.at[s], inc=1, device_id=pairs[s][1], device_id_type=MESH)
     for copy in y_copies:
         copy.start()
-    for s in range(2):
-        pl.semaphore_signal(open_sem.at[s], inc=1, device_id=pairs[s][1], device_id_type=MESH)
     pl.semaphore_signal(met_sem, inc=1, device_id=below, device_id_type=MESH)
 
     d_load.wait()
@@ -144,11 +144,11 @@
     at_home = c == 2 * HALF - 1
     for s in range(2):
         pl.semaphore_wait(open_sem.at[s], 1)
-        src_b, src_c = pairs[s][0]
-        src_base = src_c - lax.rem(src_c, HALF)
-        for i in ids + [g]:
+    bases = [pairs[s][0][1] - lax.rem(pairs[s][0][1], HALF) for s in range(2)]
+    for i in ids + [g]:
+        for s in range(2):
             src, dst = car_out.at[s, i], car_in.at[s, g]
-            copy = remote(src, dst, car_ssem, car_rsem, (src_b, src_base + i))
+            copy = remote(src, dst, car_ssem, car_rsem, (pairs[s][0][0], bases[s] + i))
             if s == 1 and i is g:
                 inside = pltpu.make_async_copy(src, dst, car_rsem)
                 pl.when(at_home)(lambda: inside.start())

time: 37.9 us -> 38.2 us (level)
  no operation moved by 1% of the time
where the time goes in v5:
time: 38.2 us; the launch traced here: 38.1 us
  Pallas kernels  37.4 us (98%)
  local copies, waits for them, and re-layouts  0.66 us (2%)
    pallas_call x1, Pallas kernels, shards(): pl.pallas_call(kernel, out_shape=pltpu.VMEM((256, 128), F32), in_specs=[h...  37.4 us

profile of v5, /device:TPU:1, one launch (start us, length us, event | category | flops | bytes accessed | tf_op | source)
XLA Modules:
  0.0 38.1 jit_solution(16989528208498311980)
XLA Ops:
  0.0 37.4 %shard_map.64 = f32[256,128]{1,0:T(8,128)S(1)} custom-call(bf16[64,512]{1,0:T(8,128)(2,1)} %bitcast.15, bf16[256,512]{1,0:T(8,128)(2,1)} %bitcast.14, bf16[8,2,2,32,512]{4,3,2,1,0:T(8,128)(2,1)} %bitcast.12, bf16[8,2,2,32,512]{4,3,2,1,0:T(8,128)(2,1)} %bitcast.13, s32[2,2,8]{2,1,0:T(2,128)} %bitcast.16, s32[2,2,8]{2,1,0:T(2,128)} %bitcast.17), custom_call_target="tpu_custom_call" | custom-call | flops 300000000 | bytes 2500000 | tf_op jit(solution)/shard_map/pallas_call | solution.py:205
  37.4 0.7 %copy.9 = f32[8,8,1,512]{3,2,1,0:T(1,128)} copy(f32[8,8,1,512]{3,2,1,0:T(1,128)S(1)} %bitcast.11) | data formatting | bytes 262144

commit v6 on v5

--- a/solution.py
+++ b/solution.py
@@ -65,7 +65,7 @@
         return copy
 
     pairs = [partners(b, c, s) for s in range(2)]
-    greet([pairs[0][0], pairs[1][0], pairs[0][1], pairs[1][1]])
+    greet([pairs[0][0], pairs[1][0]])
     small = [load(0, rank_hbm, rank_v), load(1, pres_hbm, pres_v)]
     x_load = load(2, x_hbm, x_v)
     above, below = quarter(b, c, 4), quarter(b, c, 12)
@@ -125,7 +125,7 @@
             car_tmp[s, pl.ds(k, 64, stride=4), :] = image[:, 128 * k : 128 * k + 128]
         car_out[s] = car_tmp[s].reshape(HALF, CHUNK, 128).astype(BF16)
 
-    pl.semaphore_wait(barrier, 6 + len(group))
+    pl.semaphore_wait(barrier, 4 + len(group))
     for s in range(2):
         pl.semaphore_signal(open_sem.at[s], inc=1, device_id=pairs[s][1], device_id_type=MESH)
     for copy in y_copies:

time: 38.2 us -> 38.2 us (level)
  no operation moved by 1% of the time
where the time goes in v6:
time: 38.2 us; the launch traced here: 38.1 us
  Pallas kernels  37.4 us (98%)
  local copies, waits for them, and re-layouts  0.66 us (2%)
    pallas_call x1, Pallas kernels, shards(): pl.pallas_call(kernel, out_shape=pltpu.VMEM((256, 128), F32), in_specs=[h...  37.4 us

profile of v6, /device:TPU:1, one launch (start us, length us, event | category | flops | bytes accessed | tf_op | source)
XLA Modules:
  0.0 38.1 jit_solution(16952018422984387403)
XLA Ops:
  0.0 37.4 %shard_map.64 = f32[256,128]{1,0:T(8,128)S(1)} custom-call(bf16[64,512]{1,0:T(8,128)(2,1)} %bitcast.15, bf16[256,512]{1,0:T(8,128)(2,1)} %bitcast.14, bf16[8,2,2,32,512]{4,3,2,1,0:T(8,128)(2,1)} %bitcast.12, bf16[8,2,2,32,512]{4,3,2,1,0:T(8,128)(2,1)} %bitcast.13, s32[2,2,8]{2,1,0:T(2,128)} %bitcast.16, s32[2,2,8]{2,1,0:T(2,128)} %bitcast.17), custom_call_target="tpu_custom_call" | custom-call | flops 300000000 | bytes 2500000 | tf_op jit(solution)/shard_map/pallas_call | solution.py:205
  37.4 0.7 %copy.9 = f32[8,8,1,512]{3,2,1,0:T(1,128)} copy(f32[8,8,1,512]{3,2,1,0:T(1,128)S(1)} %bitcast.11) | data formatting | bytes 262144

commit v7 on v6

--- a/solution.py
+++ b/solution.py
@@ -71,10 +71,16 @@
     above, below = quarter(b, c, 4), quarter(b, c, 12)
     g = lax.rem(c, HALF)
     base = c - g
-    far_first = (4, 5, 3, 2, 6, 7, 1)
-    ids = [lax.rem(g + o, HALF) for o in far_first]
-    group = [(b, base + i) for i in ids]
-    greet([above, below] + group)
+
+    def others_in_half(step):
+        def one(k, carry):
+            step(lax.rem(g + 1 + lax.rem(k + 3, HALF - 1), HALF))
+            return carry
+
+        lax.fori_loop(0, HALF - 1, one, 0)
+
+    greet([above, below])
+    others_in_half(lambda i: greet([(b, base + i)]))
     tiles = [
         [load(3 + 2 * s, u_hbm.at[:, :, s], u_v.at[:, :, s]), load(4 + 2 * s, v_hbm.at[:, :, s], v_v.at[:, :, s])]
         for s in range(2)
@@ -125,7 +131,7 @@
             car_tmp[s, pl.ds(k, 64, stride=4), :] = image[:, 128 * k : 128 * k + 128]
         car_out[s] = car_tmp[s].reshape(HALF, CHUNK, 128).astype(BF16)
 
-    pl.semaphore_wait(barrier, 4 + len(group))
+    pl.semaphore_wait(barrier, 4 + HALF - 1)
     for s in range(2):
         pl.semaphore_signal(open_sem.at[s], inc=1, device_id=pairs[s][1], device_id_type=MESH)
     for copy in y_copies:
@@ -145,17 +151,21 @@
     for s in range(2):
         pl.semaphore_wait(open_sem.at[s], 1)
     bases = [pairs[s][0][1] - lax.rem(pairs[s][0][1], HALF) for s in range(2)]
-    for i in ids + [g]:
+
+    def scatter(i, own):
         for s in range(2):
             src, dst = car_out.at[s, i], car_in.at[s, g]
             copy = remote(src, dst, car_ssem, car_rsem, (pairs[s][0][0], bases[s] + i))
-            if s == 1 and i is g:
+            if s == 1 and own:
                 inside = pltpu.make_async_copy(src, dst, car_rsem)
                 pl.when(at_home)(lambda: inside.start())
                 pl.when(jnp.logical_not(at_home))(lambda: copy.start())
             else:
                 copy.start()
 
+    others_in_half(lambda i: scatter(i, False))
+    scatter(g, True)
+
     for s in range(2):
         y_copies[s].wait_recv()
         a = pick(dot_t(y_v[s], section(v_v, s)), 1, s, row)
@@ -166,8 +176,7 @@
     def chunk(i):
         return pl.ds(pl.multiple_of(CHUNK * i, CHUNK), CHUNK)
 
-    for i, peer in zip(ids, group):
-        remote(rs_out.at[chunk(i)], rs_in.at[g], rs_ssem, rs_rsem, peer).start()
+    others_in_half(lambda i: remote(rs_out.at[chunk(i)], rs_in.at[g], rs_ssem, rs_rsem, (b, base + i)).start())
     rs_in[g] = rs_out[chunk(g), :]
     for copy in y_copies:
         copy.wait_send()
@@ -191,8 +200,7 @@
     zx_copy.wait_recv()
     mine = out.at[chunk(g)]
     mine[...] = part + zx_in[...]
-    for peer in group:
-        remote(mine, mine, ag_ssem, ag_rsem, peer).start()
+    others_in_half(lambda i: remote(mine, mine, ag_ssem, ag_rsem, (b, base + i)).start())
     zx_copy.wait_send()
     others = out.at[pl.ds(0, CHUNK * (HALF - 1))]
     wait_bytes(others, ag_rsem)

time: 38.2 us -> 38.2 us (level)
  no operation moved by 1% of the time
where the time goes in v7:
time: 38.2 us; the launch traced here: 38.1 us
  Pallas kernels  37.4 us (98%)
  local copies, waits for them, and re-layouts  0.66 us (2%)
    pallas_call x1, Pallas kernels, shards(): pl.pallas_call(kernel, out_shape=pltpu.VMEM((256, 128), F32), in_specs=[h...  37.4 us

profile of v7, /device:TPU:1, one launch (start us, length us, event | category | flops | bytes accessed | tf_op | source)
XLA Modules:
  0.0 38.1 jit_solution(11851985118904941369)
XLA Ops:
  0.0 37.4 %shard_map.64 = f32[256,128]{1,0:T(8,128)S(1)} custom-call(bf16[64,512]{1,0:T(8,128)(2,1)} %bitcast.15, bf16[256,512]{1,0:T(8,128)(2,1)} %bitcast.14, bf16[8,2,2,32,512]{4,3,2,1,0:T(8,128)(2,1)} %bitcast.12, bf16[8,2,2,32,512]{4,3,2,1,0:T(8,128)(2,1)} %bitcast.13, s32[2,2,8]{2,1,0:T(2,128)} %bitcast.16, s32[2,2,8]{2,1,0:T(2,128)} %bitcast.17), custom_call_target="tpu_custom_call" | custom-call | flops 300000000 | bytes 2500000 | tf_op jit(solution)/shard_map/pallas_call | solution.py:213
  37.4 0.7 %copy.9 = f32[8,8,1,512]{3,2,1,0:T(1,128)} copy(f32[8,8,1,512]{3,2,1,0:T(1,128)S(1)} %bitcast.11) | data formatting | bytes 262144

commit v8 on v3

--- a/solution.py
+++ b/solution.py
@@ -65,7 +65,7 @@
         return copy
 
     pairs = [partners(b, c, s) for s in range(2)]
-    greet([pairs[0][0], pairs[1][0], pairs[0][1], pairs[1][1]])
+    greet([pairs[0][0], pairs[1][0]])
     small = [load(0, rank_hbm, rank_v), load(1, pres_hbm, pres_v)]
     x_load = load(2, x_hbm, x_v)
     above, below = quarter(b, c, 4), quarter(b, c, 12)
@@ -125,7 +125,7 @@
             car_tmp[s, pl.ds(k, 64, stride=4), :] = image[:, 128 * k : 128 * k + 128]
         car_out[s] = car_tmp[s].reshape(HALF, CHUNK, 128).astype(BF16)
 
-    pl.semaphore_wait(barrier, 6 + len(group))
+    pl.semaphore_wait(barrier, 4 + len(group))
     for copy in y_copies:
         copy.start()
     for s in range(2):

time: 37.9 us -> 37.7 us (level)
  no operation moved by 1% of the time
where the time goes in v8:
time: 37.7 us; the launch traced here: 37.4 us
  Pallas kernels  36.8 us (98%)
  local copies, waits for them, and re-layouts  0.66 us (2%)
    pallas_call x1, Pallas kernels, shards(): pl.pallas_call(kernel, out_shape=pltpu.VMEM((256, 128), F32), in_specs=[h...  36.8 us

profile of v8, /device:TPU:1, one launch (start us, length us, event | category | flops | bytes accessed | tf_op | source)
XLA Modules:
  0.0 37.4 jit_solution(12935592323808256116)
XLA Ops:
  0.0 36.8 %shard_map.64 = f32[256,128]{1,0:T(8,128)S(1)} custom-call(bf16[64,512]{1,0:T(8,128)(2,1)} %bitcast.15, bf16[256,512]{1,0:T(8,128)(2,1)} %bitcast.14, bf16[8,2,2,32,512]{4,3,2,1,0:T(8,128)(2,1)} %bitcast.12, bf16[8,2,2,32,512]{4,3,2,1,0:T(8,128)(2,1)} %bitcast.13, s32[2,2,8]{2,1,0:T(2,128)} %bitcast.16, s32[2,2,8]{2,1,0:T(2,128)} %bitcast.17), custom_call_target="tpu_custom_call" | custom-call | flops 300000000 | bytes 2500000 | tf_op jit(solution)/shard_map/pallas_call | solution.py:205
  36.8 0.7 %copy.9 = f32[8,8,1,512]{3,2,1,0:T(1,128)} copy(f32[8,8,1,512]{3,2,1,0:T(1,128)S(1)} %bitcast.11) | data formatting | bytes 262144

commit v9 on v3

--- a/solution.py
+++ b/solution.py
@@ -123,14 +123,7 @@
         image = dot(t, section(v_v, s))
         for k in range(4):
             car_tmp[s, pl.ds(k, 64, stride=4), :] = image[:, 128 * k : 128 * k + 128]
-        car_out[s] = car_tmp[s].reshape(HALF, CHUNK, 128).astype(BF16)
-
-    pl.semaphore_wait(barrier, 6 + len(group))
-    for copy in y_copies:
-        copy.start()
-    for s in range(2):
-        pl.semaphore_signal(open_sem.at[s], inc=1, device_id=pairs[s][1], device_id_type=MESH)
-    pl.semaphore_signal(met_sem, inc=1, device_id=below, device_id_type=MESH)
+        car_out[s] = car_tmp[s, :256].reshape(HALF, CHUNK, 128).astype(BF16)
 
     d_load.wait()
     dg = dot_t(x, d_v[...]).reshape(8, 8, 256)
@@ -140,6 +133,13 @@
     dg = dg + pltpu.roll(dg, 32, 1)
     total = jnp.concatenate([dg] * 4, 1).reshape(8, 8, 512)
     total = jnp.where((lane >> 5 == c)[None], total, 0.0).reshape(64, 512)
+
+    pl.semaphore_wait(barrier, 6 + len(group))
+    for copy in y_copies:
+        copy.start()
+    for s in range(2):
+        pl.semaphore_signal(open_sem.at[s], inc=1, device_id=pairs[s][1], device_id_type=MESH)
+    pl.semaphore_signal(met_sem, inc=1, device_id=below, device_id_type=MESH)
 
     at_home = c == 2 * HALF - 1
     for s in range(2):
@@ -215,10 +215,10 @@
             pltpu.VMEM((2, 2, 8), jnp.int32),
             pltpu.VMEM((2, 2, 8), jnp.int32),
             pltpu.VMEM((2, 64, 512), BF16),
-            pltpu.VMEM((2, 256, 128), F32),
+            pltpu.VMEM((2, 264, 128), F32),
             pltpu.VMEM((2, HALF, CHUNK, 128), BF16),
             pltpu.VMEM((2, HALF, CHUNK, 128), BF16),
-            pltpu.VMEM((256, 128), F32),
+            pltpu.VMEM((264, 128), F32),
             pltpu.VMEM((HALF, CHUNK, 128), F32),
             pltpu.VMEM((CHUNK, 128), F32),
             pltpu.VMEM((CHUNK, 128), F32),

time: 37.9 us -> 37.9 us (level)
  no operation moved by 1% of the time
where the time goes in v9:
time: 37.9 us; the launch traced here: 37.8 us
  Pallas kernels  37.1 us (98%)
  local copies, waits for them, and re-layouts  0.66 us (2%)
    pallas_call x1, Pallas kernels, shards(): pl.pallas_call(kernel, out_shape=pltpu.VMEM((256, 128), F32), in_specs=[h...  37.1 us

profile of v9, /device:TPU:1, one launch (start us, length us, event | category | flops | bytes accessed | tf_op | source)
XLA Modules:
  0.0 37.8 jit_solution(1807042558433441934)
XLA Ops:
  0.0 37.1 %shard_map.64 = f32[256,128]{1,0:T(8,128)S(1)} custom-call(bf16[64,512]{1,0:T(8,128)(2,1)} %bitcast.15, bf16[256,512]{1,0:T(8,128)(2,1)} %bitcast.14, bf16[8,2,2,32,512]{4,3,2,1,0:T(8,128)(2,1)} %bitcast.12, bf16[8,2,2,32,512]{4,3,2,1,0:T(8,128)(2,1)} %bitcast.13, s32[2,2,8]{2,1,0:T(2,128)} %bitcast.16, s32[2,2,8]{2,1,0:T(2,128)} %bitcast.17), custom_call_target="tpu_custom_call" | custom-call | flops 300000000 | bytes 2500000 | tf_op jit(solution)/shard_map/pallas_call | solution.py:205
  37.1 0.7 %copy.9 = f32[8,8,1,512]{3,2,1,0:T(1,128)} copy(f32[8,8,1,512]{3,2,1,0:T(1,128)S(1)} %bitcast.11) | data formatting | bytes 262144
